TPU v7x, 32 devices: a whole 2x2x4 slice. The times are simulated.
32 devices in a mesh: dp: 2 (over x), seq: 16 (over z, y, core).
Axes of the slice: x: 2, y: 2, z: 4, core: 2. Of those that a mesh axis runs over, the one named last changes fastest.
Arguments:
- queries: bfloat16 [2, 2048, 1024], P('dp', 'seq'), may hold values from -6 to 6
- keys: bfloat16 [2, 2048, 1024], P('dp', 'seq'), may hold values from -6 to 6
- values: bfloat16 [2, 2048, 1024], P('dp', 'seq'), may hold values from -6 to 6
- grad_out: bfloat16 [2, 2048, 1024], P('dp', 'seq'), may hold values from -6 to 6
- mem_keys: bfloat16 [16, 512, 1024], P('dp', 'seq'), may hold values from -6 to 6
- mem_values: bfloat16 [16, 512, 1024], P('dp', 'seq'), may hold values from -6 to 6
- seq_lengths: int32 [2], replicated, may hold values from 256 to 2048, as said below
- mem_counts: int32 [2], replicated, may hold values from 1 to 4, as said below
- block_lists: int32 [2, 4], replicated, may hold values from 0 to 15, as said below
- block_slots: int32 [16], replicated, may hold values from 0 to 15, each once
Outputs:
- grad_queries: bfloat16 [2, 2048, 1024], P('dp', 'seq')
- grad_keys: bfloat16 [2, 2048, 1024], P('dp', 'seq')
- grad_values: bfloat16 [2, 2048, 1024], P('dp', 'seq')
Inputs may be any that keep to these rules, and one draw needn't show every extreme that they name: `seq_lengths`: some user has all 2048 events. `mem_counts`: some user attends to all 4 listed blocks. `block_lists`: the 4 ids of one user are distinct. `block_slots`: A permutation of the block ids.
All inputs are finite; a program needn't handle non-finite values.
Results may differ from a plain program's by a relative error of at most 0.0063.
Values may be sent and summed in bfloat16 or wider, within the bound.
No kernel may reach another device: no remote copies, remote signals or barrier semaphores. Data moves between devices by JAX's collectives and lax.ppermute only.
A program may use at most 128 MiB of HBM per device.

v0:
```python
import math

import jax
import jax.numpy as jnp
from jax import lax
from jax.sharding import PartitionSpec as P

H = 8
WINDOW = 512


def passed_along(value, axis, by):
    count = lax.axis_size(axis)
    pairs = [(i, i + by) for i in range(count) if 0 <= i + by < count]
    return lax.ppermute(value, axis, pairs)


def head_terms(query_h, key_h, value_h, grad_h, memk_h, memv_h, allow_window, allow_memory):
    scaling = 1.0 / math.sqrt(query_h.shape[1])
    score_w = jnp.dot(query_h, key_h.T, preferred_element_type=jnp.float32) * scaling
    score_m = jnp.dot(query_h, memk_h.T, preferred_element_type=jnp.float32) * scaling
    score_w = jnp.where(allow_window, score_w, -1e30)
    score_m = jnp.where(allow_memory, score_m, -1e30)
    row_top = jnp.maximum(jnp.max(score_w, axis=1), jnp.max(score_m, axis=1))
    expo_w = jnp.exp(score_w - row_top[:, None])
    expo_m = jnp.exp(score_m - row_top[:, None])
    totals = jnp.sum(expo_w, axis=1) + jnp.sum(expo_m, axis=1)
    prob_w = expo_w / totals[:, None]
    prob_m = expo_m / totals[:, None]
    half_w = prob_w.astype(jnp.bfloat16)
    half_m = prob_m.astype(jnp.bfloat16)
    output = jnp.dot(half_w, value_h, preferred_element_type=jnp.float32) + jnp.dot(
        half_m, memv_h, preferred_element_type=jnp.float32
    )
    deltas = jnp.sum(grad_h.astype(jnp.float32) * output, axis=1)
    dprob_w = jnp.dot(grad_h, value_h.T, preferred_element_type=jnp.float32)
    dprob_m = jnp.dot(grad_h, memv_h.T, preferred_element_type=jnp.float32)
    dscore_w = (prob_w * (dprob_w - deltas[:, None])).astype(jnp.bfloat16)
    dscore_m = (prob_m * (dprob_m - deltas[:, None])).astype(jnp.bfloat16)
    grad_query = (
        jnp.dot(dscore_w, key_h, preferred_element_type=jnp.float32)
        + jnp.dot(dscore_m, memk_h, preferred_element_type=jnp.float32)
    ) * scaling
    grad_key = jnp.dot(dscore_w.T, query_h, preferred_element_type=jnp.float32) * scaling
    grad_value = jnp.dot(half_w.T, grad_h, preferred_element_type=jnp.float32)
    return (grad_query, grad_key, grad_value, row_top, totals, deltas)


def combine_heads(stacked):
    return jnp.transpose(stacked, (1, 0, 2)).reshape(
        stacked.shape[1], stacked.shape[0] * stacked.shape[2]
    )


def all_heads(
    query_rows, key_rows, value_rows, grad_rows, memk_rows, memv_rows, allow_window, allow_memory
):
    width = query_rows.shape[1] // H

    def per_head(index):

        def column_slice(tensor):
            return lax.dynamic_slice_in_dim(tensor, index * width, width, 1)

        return head_terms(
            column_slice(query_rows),
            column_slice(key_rows),
            column_slice(value_rows),
            column_slice(grad_rows),
            column_slice(memk_rows),
            column_slice(memv_rows),
            allow_window,
            allow_memory,
        )

    grad_query, grad_key, grad_value, row_top, totals, deltas = lax.map(
        per_head, jnp.arange(H, dtype=jnp.int32)
    )
    return (
        combine_heads(grad_query),
        combine_heads(grad_key),
        combine_heads(grad_value),
        jnp.stack([row_top, totals, deltas]),
    )


def on_device(
    queries,
    keys,
    values,
    grad_out,
    mem_keys,
    mem_values,
    seq_lengths,
    mem_counts,
    block_lists,
    block_slots,
):
    rows = queries.shape[1]
    width = queries.shape[2]
    reach = WINDOW // rows
    shard = lax.axis_index("seq")
    owner_me = lax.axis_index("dp")
    length = lax.dynamic_index_in_dim(seq_lengths, owner_me, 0, keepdims=False)
    count = lax.dynamic_index_in_dim(mem_counts, owner_me, 0, keepdims=False)
    own_pair = jnp.stack([keys[0], values[0]])
    earlier = [passed_along(own_pair, "seq", offset) for offset in range(1, reach + 1)]
    window_pair = jnp.concatenate(earlier[::-1] + [own_pair], axis=1)
    pool_pair = jnp.stack([mem_keys, mem_values])
    block_range = jnp.arange(block_slots.shape[0], dtype=jnp.int32)
    slot_table = jnp.sum(
        jnp.where(
            block_range[None, None, :] == block_lists[:, :, None], block_slots[None, None, :], 0
        ),
        axis=2,
    )
    whole_pool = lax.all_gather(pool_pair, "dp", axis=1, tiled=True)
    my_slots = lax.dynamic_index_in_dim(slot_table, owner_me, 0, keepdims=False)
    chosen = jnp.take(whole_pool, my_slots, axis=1)
    memory_pair = lax.all_gather(chosen, "seq", axis=2, tiled=True)
    memory_pair = memory_pair.reshape(2, memory_pair.shape[1] * memory_pair.shape[2], width)
    memory_events = memory_pair.shape[1]
    block_size = memory_events // chosen.shape[1]
    query_pos = shard * rows + jnp.arange(rows, dtype=jnp.int32)
    key_pos = (shard - reach) * rows + jnp.arange((reach + 1) * rows, dtype=jnp.int32)
    allow_window = (
        (key_pos[None, :] <= query_pos[:, None])
        & (query_pos[:, None] - key_pos[None, :] < WINDOW)
        & (key_pos[None, :] >= 0)
        & ((key_pos[None, :] < length) | (key_pos[None, :] == query_pos[:, None]))
    )
    allow_memory = (jnp.arange(memory_events, dtype=jnp.int32) // block_size < count)[None, :]
    masked = grad_out[0] * (query_pos < length)[:, None].astype(jnp.bfloat16)
    grad_query, grad_key, grad_value, row_stats = all_heads(
        queries[0],
        window_pair[0],
        window_pair[1],
        masked,
        memory_pair[0],
        memory_pair[1],
        allow_window,
        allow_memory,
    )
    grad_pair = jnp.stack([grad_key, grad_value])
    totals = grad_pair[:, reach * rows :]
    for back in range(1, reach + 1):
        piece = grad_pair[:, (reach - back) * rows : (reach - back + 1) * rows]
        totals = totals + passed_along(piece, "seq", -back)
    return (
        grad_query.astype(jnp.bfloat16)[None],
        totals[0].astype(jnp.bfloat16)[None],
        totals[1].astype(jnp.bfloat16)[None],
    )


def solution(mesh):
    placed = (
        P("dp", "seq", None),
        P("dp", "seq", None),
        P("dp", "seq", None),
        P("dp", "seq", None),
        P("dp", "seq", None),
        P("dp", "seq", None),
        P(),
        P(),
        P(),
        P(),
    )
    return jax.shard_map(
        on_device,
        mesh=mesh,
        in_specs=placed,
        out_specs=(P("dp", "seq", None), P("dp", "seq", None), P("dp", "seq", None)),
        check_vma=False,
    )
```

profile of v0, /device:TPU:4, one launch (start us, length us, event | category | flops | bytes accessed | tf_op | source)
XLA Modules:
  0.0 375.5 jit_solution(11569284050300641531)
XLA Ops:
  7.2 2.3 pad_maximum_fusion
  10.0 34.1 %all-gather.3.cloned.1.call-done = bf16[2,16,32,1024]{3,2,1,0:T(8,128)(2,1)} async-done(((bf16[2,8,32,1024]{3,2,1,0:T(8,128)(2,1)}), bf16[2,16,32,1024]{3,2,1,0:T(8,128)(2,1)}) %all-gather.3.cloned.1.call-update) | async-done | bytes 2097168 | tf_op jit(solution)/shard_map/all_gather | solution.py:117
  44.1 2.2 gather_fusion
  48.7 1.9 collective-permute-start.3
  50.6 3.4 collective-permute-start.2
  54.0 4.3 %collective-permute-start.1 = (bf16[2,128,1024]{2,1,0:T(8,128)(2,1)}, bf16[2,128,1024]{2,1,0:T(8,128)(2,1)S(1)}, u32[]{:S(2)}, u32[]{:S(2)}) collective-permute-start(bf16[2,128,1024]{2,1,0:T(8,128)(2,1)} %constant_dynamic-update-slice_fusion), channel_id=1, source_target_pairs={{0,3},{1,4},{2,5},{3,6},{4,7},{5,8},{6,9},{7,10},{8,11},{9,12},{10... | collective-permute-start | bytes 1572872 | tf_op jit(solution)/shard_map/ppermute | solution.py:15
  58.3 3.4 collective-permute-start
  64.5 51.0 %collective-permute-done = bf16[2,128,1024]{2,1,0:T(8,128)(2,1)S(1)} collective-permute-done((bf16[2,128,1024]{2,1,0:T(8,128)(2,1)}, bf16[2,128,1024]{2,1,0:T(8,128)(2,1)S(1)}, u32[]{:S(2)}, u32[]{:S(2)}) %collective-permute-start) | collective-permute-done | bytes 524320 | tf_op jit(solution)/shard_map/ppermute | solution.py:15
  117.1 26.0 %all-gather.5.cloned.1.call-done = bf16[2,4,512,1024]{3,2,0,1:T(8,128)(2,1)} async-done(((bf16[2,4,32,1024]{3,2,0,1:T(8,128)(2,1)}), bf16[2,4,512,1024]{3,2,0,1:T(8,128)(2,1)}) %all-gather.5.cloned.1.call-update) | async-done | bytes 8388624 | tf_op jit(solution)/shard_map/all_gather | solution.py:120
  143.1 5.9 %fusion.72 = (bf16[1,4,512,1024]{3,2,0,1:T(8,128)(2,1)}, bf16[1,4,512,1024]{3,2,0,1:T(8,128)(2,1)}) fusion(bf16[2,4,512,1024]{3,2,0,1:T(8,128)(2,1)} %all-gather.5.cloned.1.call-done), kind=kLoop, calls=%fused_computation.106 | loop fusion | bytes 16777216 | tf_op jit(solution)/shard_map/slice | solution.py:140
  149.0 114.9 %while.15 = (s32[]{:T(128)}, bf16[8,128,128]{2,1,0:T(8,128)(2,1)}, f32[8,640,128]{2,1,0:T(8,128)}, f32[8,640,128]{2,1,0:T(8,128)}, s32[8]{0:T(128)S(1)}, /*index...) while((s32[]{:T(128)}, bf16[8,128,128]{2,1,0:T(8,128)(2,1)}, ...), condition=%wide.region_7.8_spmd.clone, body=%wide.region_1.7_spmd.clone.sunk | while | flops 399836800 | bytes 10319123 | solution.py:76
  158.1 2.4 fusion.126
  172.5 2.4 fusion.126
  186.9 2.4 fusion.126
  201.2 2.4 fusion.126
  215.6 2.4 fusion.126
  230.0 2.4 fusion.126
  244.3 2.4 fusion.126
  258.7 2.4 fusion.126
  263.9 4.8 %copy.20 = f32[640,8,128]{2,1,0:T(8,128)} copy(f32[640,8,128]{2,0,1:T(8,128)} %bitcast.55) | data formatting | bytes 5242880 | tf_op jit(solution)/shard_map/transpose | solution.py:50
  268.7 2.6 stack_reshape.7
  271.3 4.8 %copy.19 = f32[640,8,128]{2,1,0:T(8,128)} copy(f32[640,8,128]{2,0,1:T(8,128)} %bitcast.56) | data formatting | bytes 5242880 | tf_op jit(solution)/shard_map/transpose | solution.py:50
  276.0 3.7 stack_reshape.6
  279.8 1.9 constant_dynamic-update-slice_fusion.9
  282.0 2.0 fusion.73
  285.7 1.9 collective-permute-start.4
  290.2 1.9 collective-permute-start.5
  293.1 15.2 %collective-permute-done.4 = f32[2,128,1024]{2,1,0:T(8,128)S(1)} collective-permute-done((f32[2,128,1024]{2,1,0:T(8,128)}, f32[2,128,1024]{2,1,0:T(8,128)S(1)}, u32[]{:S(2)}, u32[]{:S(2)}) %collective-permute-start.4) | collective-permute-done | bytes 1048608 | tf_op jit(solution)/shard_map/ppermute | solution.py:15
  308.3 9.5 %collective-permute-done.7 = f32[2,128,1024]{2,1,0:T(8,128)S(1)} collective-permute-done((f32[2,128,1024]{2,1,0:T(8,128)}, f32[2,128,1024]{2,1,0:T(8,128)S(1)}, u32[]{:S(2)}, u32[]{:S(2)}) %collective-permute-start.7) | collective-permute-done | bytes 1048608 | tf_op jit(solution)/shard_map/ppermute | solution.py:15
  317.8 9.4 %collective-permute-done.6 = f32[2,128,1024]{2,1,0:T(8,128)S(1)} collective-permute-done((f32[2,128,1024]{2,1,0:T(8,128)}, f32[2,128,1024]{2,1,0:T(8,128)S(1)}, u32[]{:S(2)}, u32[]{:S(2)}) %collective-permute-start.6) | collective-permute-done | bytes 1048608 | tf_op jit(solution)/shard_map/ppermute | solution.py:15
  327.2 38.7 %collective-permute-done.5 = f32[2,128,1024]{2,1,0:T(8,128)} collective-permute-done((f32[2,128,1024]{2,1,0:T(8,128)}, f32[2,128,1024]{2,1,0:T(8,128)}, u32[]{:S(2)}, u32[]{:S(2)}) %collective-permute-start.5) | collective-permute-done | bytes 1048608 | tf_op jit(solution)/shard_map/ppermute | solution.py:15
  365.9 2.0 fusion.66
  (169 shorter events, 103.7 us)
Async XLA Ops:
  7.2 2.5 copy-start.6
  7.2 2.5 copy-start.5
  7.2 36.9 %all-gather.3.cloned.1.call-start = ((), (), s32[]{:S(2)}) async-start(), calls=%async_computation | async-start | bytes 3145728 | tf_op jit(solution)/shard_map/all_gather | solution.py:117
  7.2 40.0 %copy-start.1 = (bf16[1,128,1024]{2,1,0:T(8,128)(2,1)S(1)}, bf16[1,128,1024]{2,1,0:T(8,128)(2,1)}, u32[]{:S(2)}) copy-start(bf16[1,128,1024]{2,1,0:T(8,128)(2,1)} %param.13) | copy-start | bytes 786436
  9.6 38.4 %copy-start.2 = (bf16[1,128,1024]{2,1,0:T(8,128)(2,1)S(1)}, bf16[1,128,1024]{2,1,0:T(8,128)(2,1)}, u32[]{:S(2)}) copy-start(bf16[1,128,1024]{2,1,0:T(8,128)(2,1)} %param.14) | copy-start | bytes 786436
  9.6 52.2 %copy-start.7 = (s32[2]{0:T(128)S(1)}, s32[2]{0:T(128)}, u32[]{:S(2)}) copy-start(s32[2]{0:T(128)} %param.18) | copy-start | bytes 28
  9.6 52.8 %copy-start.3 = (bf16[1,128,1024]{2,1,0:T(8,128)(2,1)S(1)}, bf16[1,128,1024]{2,1,0:T(8,128)(2,1)}, u32[]{:S(2)}) copy-start(bf16[1,128,1024]{2,1,0:T(8,128)(2,1)} %param.15) | copy-start | bytes 786436
  9.6 54.3 %copy-start.8 = (s32[2]{0:T(128)S(1)}, s32[2]{0:T(128)}, u32[]{:S(2)}) copy-start(s32[2]{0:T(128)} %param.19) | copy-start | bytes 28
  9.6 133.5 %all-gather.5.cloned.1.call-start = ((), (), s32[]{:S(2)}) async-start(), calls=%async_computation.1 | async-start | bytes 8912896 | tf_op jit(solution)/shard_map/all_gather | solution.py:120
  48.7 66.9 %collective-permute-start.3 = (bf16[2,128,1024]{2,1,0:T(8,128)(2,1)}, bf16[2,128,1024]{2,1,0:T(8,128)(2,1)S(1)}, u32[]{:S(2)}, u32[]{:S(2)}) collective-permute-start(bf16[2,128,1024]{2,1,0:T(8,128)(2,1)} %constant_dynamic-update-slice_fusion), channel_id=1, source_target_pairs={{0,1},{1,2},{2,3},{3,4},{4,5},{5,6},{6,7},{7,8},{8,9},{9,10},{10,1... | collective-permute-start | bytes 1572872 | tf_op jit(solution)/shard_map/ppermute | solution.py:15
  50.6 65.0 %collective-permute-start.2 = (bf16[2,128,1024]{2,1,0:T(8,128)(2,1)}, bf16[2,128,1024]{2,1,0:T(8,128)(2,1)S(1)}, u32[]{:S(2)}, u32[]{:S(2)}) collective-permute-start(bf16[2,128,1024]{2,1,0:T(8,128)(2,1)} %constant_dynamic-update-slice_fusion), channel_id=1, source_target_pairs={{0,2},{1,3},{2,4},{3,5},{4,6},{5,7},{6,8},{7,9},{8,10},{9,11},{10,... | collective-permute-start | bytes 1572872 | tf_op jit(solution)/shard_map/ppermute | solution.py:15
  54.0 61.5 %collective-permute-start.1 = (bf16[2,128,1024]{2,1,0:T(8,128)(2,1)}, bf16[2,128,1024]{2,1,0:T(8,128)(2,1)S(1)}, u32[]{:S(2)}, u32[]{:S(2)}) collective-permute-start(bf16[2,128,1024]{2,1,0:T(8,128)(2,1)} %constant_dynamic-update-slice_fusion), channel_id=1, source_target_pairs={{0,3},{1,4},{2,5},{3,6},{4,7},{5,8},{6,9},{7,10},{8,11},{9,12},{10... | collective-permute-start | bytes 1572872 | tf_op jit(solution)/shard_map/ppermute | solution.py:15
  58.3 57.2 %collective-permute-start = (bf16[2,128,1024]{2,1,0:T(8,128)(2,1)}, bf16[2,128,1024]{2,1,0:T(8,128)(2,1)S(1)}, u32[]{:S(2)}, u32[]{:S(2)}) collective-permute-start(bf16[2,128,1024]{2,1,0:T(8,128)(2,1)} %constant_dynamic-update-slice_fusion), channel_id=1, source_target_pairs={{0,4},{1,5},{2,6},{3,7},{4,8},{5,9},{6,10},{7,11},{8,12},{9,13},{1... | collective-permute-start | bytes 1572872 | tf_op jit(solution)/shard_map/ppermute | solution.py:15
  282.0 3.7 copy-start
  282.0 10.1 %copy-start.4 = (bf16[8,128,128]{2,1,0:T(8,128)(2,1)S(1)}, bf16[8,128,128]{2,1,0:T(8,128)(2,1)}, u32[]{:S(2)}) copy-start(bf16[8,128,128]{2,1,0:T(8,128)(2,1)} %get-tuple-element.72) | copy-start | bytes 786436
  285.7 22.7 %collective-permute-start.4 = (f32[2,128,1024]{2,1,0:T(8,128)}, f32[2,128,1024]{2,1,0:T(8,128)S(1)}, u32[]{:S(2)}, u32[]{:S(2)}) collective-permute-start(f32[2,128,1024]{2,1,0:T(8,128)} %get-tuple-element.153), channel_id=1, source_target_pairs={{1,0},{2,1},{3,2},{4,3},{5,4},{6,5},{7,6},{8,7},{9,8},{10,9},{11,1... | collective-permute-start | bytes 3145736 | tf_op jit(solution)/shard_map/ppermute | solution.py:15
  287.6 30.2 %collective-permute-start.7 = (f32[2,128,1024]{2,1,0:T(8,128)}, f32[2,128,1024]{2,1,0:T(8,128)S(1)}, u32[]{:S(2)}, u32[]{:S(2)}) collective-permute-start(f32[2,128,1024]{2,1,0:T(8,128)} %get-tuple-element.154), channel_id=1, source_target_pairs={{4,0},{5,1},{6,2},{7,3},{8,4},{9,5},{10,6},{11,7},{12,8},{13,9},{1... | collective-permute-start | bytes 3145736 | tf_op jit(solution)/shard_map/ppermute | solution.py:15
  288.9 38.3 %collective-permute-start.6 = (f32[2,128,1024]{2,1,0:T(8,128)}, f32[2,128,1024]{2,1,0:T(8,128)S(1)}, u32[]{:S(2)}, u32[]{:S(2)}) collective-permute-start(f32[2,128,1024]{2,1,0:T(8,128)} %get-tuple-element.155), channel_id=1, source_target_pairs={{3,0},{4,1},{5,2},{6,3},{7,4},{8,5},{9,6},{10,7},{11,8},{12,9},{13... | collective-permute-start | bytes 3145736 | tf_op jit(solution)/shard_map/ppermute | solution.py:15
  290.2 75.7 %collective-permute-start.5 = (f32[2,128,1024]{2,1,0:T(8,128)}, f32[2,128,1024]{2,1,0:T(8,128)}, u32[]{:S(2)}, u32[]{:S(2)}) collective-permute-start(f32[2,128,1024]{2,1,0:T(8,128)} %get-tuple-element.156), channel_id=1, source_target_pairs={{2,0},{3,1},{4,2},{5,3},{6,4},{7,5},{8,6},{9,7},{10,8},{11,9},{12,... | collective-permute-start | bytes 3145736 | tf_op jit(solution)/shard_map/ppermute | solution.py:15
Sparse Core Ops, SparseCore 0:
  9.7 34.3 all-gather.2
  47.4 95.6 all-gather.4
where the time goes:
time: 378 us; the launch traced here: 376 us
  waiting for transfers between devices  184 us (49%)
  matrix products  95 us (25%)
  local copies, waits for them, and re-layouts  40.9 us (11%)
  starting transfers between devices  19.5 us (5%)
  other arithmetic  16.5 us (4%)
  between operations  14.4 us (4%)
  loops' own time  5.42 us (1%)
    ppermute x8, waiting for transfers between devices, passed_along(): return lax.ppermute(value, axis, pairs)  124 us
    all_gather x1, waiting for transfers between devices, on_device(): whole_pool = lax.all_gather(pool_pair, 'dp', axis=1, tiled=True)  34.1 us
    all_gather x1, waiting for transfers between devices, on_device(): memory_pair = lax.all_gather(chosen, 'seq', axis=2, tiled=True)  26 us
    ppermute x8, starting transfers between devices, passed_along(): return lax.ppermute(value, axis, pairs)  19.4 us
    dot_general x8, matrix products, head_terms(): jnp.dot(dscore_m, memk_h, preferred_element_type=jnp.float32)  19.2 us
    dot_general x8, matrix products, head_terms(): jnp.dot(dscore_w.T, query_h, preferred_element_type=jnp.float32) * scaling  13.8 us
    dot_general x8, matrix products, head_terms(): jnp.dot(half_m, memv_h, preferred_element_type=jnp.float32)  12.2 us
    dot_general x8, matrix products, head_terms(): jnp.dot(query_h, memk_h.T, preferred_element_type=jnp.float32) * scaling  11.6 us
  transfers between devices with their start and end apart: 10, of which 7 were waited for; matrix products, arithmetic and copies ran while one was open for 2% of the time, Pallas kernels for 0%

commit v1 on v0

v1 whole, which is shorter than its diff:
```python
import functools
import math

import jax
import jax.numpy as jnp
from jax import lax
from jax.experimental import pallas as pl
from jax.experimental.pallas import tpu as pltpu
from jax.sharding import PartitionSpec as P

H = 8
WINDOW = 512
TILE = 256
NEG = -1e30
LOG2E = 1.4426950408889634
VMEM_LIMIT = 48 * 1024 * 1024
VMEM_WHOLE = 64 * 1024 * 1024 - 256 * 1024

NT = (((1,), (1,)), ((), ()))
TN = (((0,), (0,)), ((), ()))


def dot_nt(a, b):
    return lax.dot_general(a, b, NT, preferred_element_type=jnp.float32)


def dot_tn(a, b):
    return lax.dot_general(a, b, TN, preferred_element_type=jnp.float32)


def dot_nn(a, b):
    return jnp.dot(a, b, preferred_element_type=jnp.float32)


def call(body, limit=VMEM_LIMIT, **kw):
    return pl.pallas_call(
        body, compiler_params=pltpu.CompilerParams(vmem_limit_bytes=limit), **kw
    )


def pack_body(slots_ref, lists_ref, q_ref, k_ref, v_ref, g_ref, mk_ref, mv_ref, rows_ref, edge_ref, sems):
    users, blocks = rows_ref.shape[0] + 1, rows_ref.shape[1]
    held = mk_ref.shape[0]
    user = lax.axis_index("dp")
    early = lax.rem(lax.axis_index("seq"), H) < WINDOW // q_ref.shape[1]
    copies = []
    for step in range(1, users):
        other = lax.rem(user + step, users)
        for block in range(blocks):
            index = lax.rem(slots_ref[lists_ref[other, block]], held)
            for part, pool in enumerate((mk_ref, mv_ref)):
                copies.append((pool.at[index], rows_ref.at[step - 1, block, part]))
    copies = [
        pltpu.make_async_copy(src, dst, sems.at[i]) for i, (src, dst) in enumerate(copies)
    ]
    for copy in copies:
        copy.start()
    last = len(copies)

    @pl.when(early)
    def _():
        for part, ref in enumerate((q_ref, g_ref)):
            pltpu.make_async_copy(ref.at[0], edge_ref.at[part], sems.at[last + part]).start()

    @pl.when(jnp.logical_not(early))
    def _():
        for part, ref in enumerate((k_ref, v_ref)):
            pltpu.make_async_copy(ref.at[0], edge_ref.at[part], sems.at[last + part]).start()

    for copy in copies:
        copy.wait()
    for part in range(2):
        pltpu.make_async_copy(q_ref.at[0], edge_ref.at[part], sems.at[last + part]).wait()


def pack(users, block_slots, block_lists, queries, keys, values, grad_out, mem_keys, mem_values):
    _, rows, width = queries.shape
    _, depth, _ = mem_keys.shape
    blocks = block_lists.shape[1]
    smem = pl.BlockSpec(memory_space=pltpu.SMEM)
    hbm = pl.BlockSpec(memory_space=pltpu.HBM)
    return call(
        pack_body,
        limit=VMEM_WHOLE,
        in_specs=[smem] * 2 + [hbm] * 6,
        out_specs=[hbm] * 2,
        out_shape=[
            jax.ShapeDtypeStruct((users - 1, blocks, 2, depth, width), mem_keys.dtype),
            jax.ShapeDtypeStruct((2, rows, width), queries.dtype),
        ],
        scratch_shapes=[pltpu.SemaphoreType.DMA(((users - 1) * blocks * 2 + 2,))],
    )(block_slots, block_lists, queries, keys, values, grad_out, mem_keys, mem_values)


def memory_body(hd, slots_ref, lists_ref, mk_ref, mv_ref, *refs):
    received, out_ref, buffer, sems = refs[:-3], refs[-3], refs[-2], refs[-1]
    users, blocks, depth = len(received) + 1, buffer.shape[0], buffer.shape[2]
    held = mk_ref.shape[0]
    user = lax.axis_index("dp")
    for block in range(blocks):
        slot = slots_ref[lists_ref[user, block]]
        source = lax.rem(user - slot // held + users, users)
        for step in range(users):

            @pl.when(source == step)
            def _():
                for part, pool in enumerate((mk_ref, mv_ref)):
                    if step == 0:
                        src = pool.at[lax.rem(slot, held)]
                    else:
                        src = received[step - 1].at[0, block, part]
                    pltpu.make_async_copy(src, buffer.at[block, part], sems.at[block, part]).start()

    for block in range(blocks):
        for part in range(2):
            pltpu.make_async_copy(mk_ref.at[0], buffer.at[block, part], sems.at[block, part]).wait()
            rows = buffer[block, part]
            for piece in range(out_ref.shape[0]):
                head = piece % H
                out_ref[piece, part, block * depth : (block + 1) * depth] = rows[
                    :, head * hd : (head + 1) * hd
                ]


def memory_pieces(block_slots, block_lists, mem_keys, mem_values, got, pieces):
    _, depth, width = mem_keys.shape
    blocks = block_lists.shape[1]
    hd = width // H
    smem = pl.BlockSpec(memory_space=pltpu.SMEM)
    hbm = pl.BlockSpec(memory_space=pltpu.HBM)
    anywhere = pl.BlockSpec(memory_space=pl.ANY)
    return call(
        functools.partial(memory_body, hd),
        limit=VMEM_WHOLE,
        in_specs=[smem] * 2 + [hbm] * 2 + [anywhere] * len(got),
        out_specs=pl.BlockSpec(memory_space=pltpu.VMEM),
        out_shape=jax.ShapeDtypeStruct((pieces, 2, blocks * depth, hd), mem_keys.dtype),
        scratch_shapes=[
            pltpu.VMEM((blocks, 2, depth, width), mem_keys.dtype),
            pltpu.SemaphoreType.DMA((blocks, 2)),
        ],
    )(block_slots, block_lists, mem_keys, mem_values, *got)


def split_body(hd, length_ref, *refs):
    sources, out_ref, buffer, sems = refs[:4], refs[4], refs[5], refs[6]
    rows = buffer.shape[1]
    copies = [
        pltpu.make_async_copy(source.at[0], buffer.at[part], sems.at[part])
        for part, source in enumerate(sources)
    ]
    for copy in copies:
        copy.start()
    live = length_ref[lax.axis_index("dp")] - lax.axis_index("seq") * rows
    position = lax.broadcasted_iota(jnp.int32, (rows, hd), 0)
    for part, copy in enumerate(copies):
        copy.wait()
        for head in range(H):
            block = buffer[part, :, head * hd : (head + 1) * hd]
            if part == 3:
                block = jnp.where(position < live, block.astype(jnp.float32), 0.0)
            out_ref[head, part] = block.astype(out_ref.dtype)


def split_heads(seq_lengths, *arrays):
    _, rows, width = arrays[0].shape
    hd = width // H
    parts = len(arrays)
    return call(
        functools.partial(split_body, hd),
        limit=VMEM_WHOLE,
        in_specs=[pl.BlockSpec(memory_space=pltpu.SMEM)]
        + [pl.BlockSpec(memory_space=pltpu.HBM)] * parts,
        out_specs=pl.BlockSpec(memory_space=pltpu.VMEM),
        out_shape=jax.ShapeDtypeStruct((H, parts, rows, hd), arrays[0].dtype),
        scratch_shapes=[
            pltpu.VMEM((parts, rows, width), arrays[0].dtype),
            pltpu.SemaphoreType.DMA((parts,)),
        ],
    )(seq_lengths, *arrays)


def edge_body(hd, length_ref, in_ref, _, out_ref):
    rows = in_ref.shape[1]
    reach = WINDOW // rows
    shard = lax.axis_index("seq")
    beyond = length_ref[lax.axis_index("dp")] - (shard + reach) * rows
    live = jnp.where(lax.rem(shard, H) < reach, rows, beyond)
    position = lax.broadcasted_iota(jnp.int32, (rows, hd), 0)
    for head in range(H):
        cols = slice(head * hd, (head + 1) * hd)
        out_ref[head, 0] = in_ref[0, :, cols]
        grad = in_ref[1, :, cols].astype(jnp.float32)
        out_ref[head, 1] = jnp.where(position < live, grad, 0.0).astype(out_ref.dtype)


def split_edge(seq_lengths, edge, later_than):
    _, rows, width = edge.shape
    hd = width // H
    vmem = pl.BlockSpec(memory_space=pltpu.VMEM)
    return call(
        functools.partial(edge_body, hd),
        in_specs=[
            pl.BlockSpec(memory_space=pltpu.SMEM),
            vmem,
            pl.BlockSpec(memory_space=pl.ANY),
        ],
        out_specs=vmem,
        out_shape=jax.ShapeDtypeStruct((H, 2, rows, hd), edge.dtype),
    )(seq_lengths, edge, later_than)


def attend_body(
    scale,
    depth,
    half,
    length_ref,
    count_ref,
    ev_ref,
    edge_ref,
    mem_ref,
    gq_ref,
    gk_ref,
    gv_ref,
    *refs,
):
    k_all, v_all = refs[-2:]
    step = pl.program_id(0)
    hd = ev_ref.shape[-1]
    rows = ev_ref.shape[2]
    reach = WINDOW // rows
    user = lax.axis_index("dp")
    length, count = length_ref[user], count_ref[user]
    base = (lax.axis_index("seq") // H) * (H * rows) + half * WINDOW
    slope = scale * LOG2E
    blocks_per_tile = TILE // rows

    @pl.when(step == 0)
    def _():
        if half == 0:
            k_all[:WINDOW] = edge_ref[:reach, 0].reshape(WINDOW, hd)
            v_all[:WINDOW] = edge_ref[:reach, 1].reshape(WINDOW, hd)
        else:
            k_all[:WINDOW] = ev_ref[:reach, 1].reshape(WINDOW, hd)
            v_all[:WINDOW] = ev_ref[:reach, 2].reshape(WINDOW, hd)
        own = slice(half * reach, (half + 1) * reach)
        k_all[WINDOW:] = ev_ref[own, 1].reshape(WINDOW, hd)
        v_all[WINDOW:] = ev_ref[own, 2].reshape(WINDOW, hd)
        gk_ref[...] = jnp.zeros_like(gk_ref)
        gv_ref[...] = jnp.zeros_like(gv_ref)

    span = WINDOW + TILE
    here = pl.ds(half * reach + step * blocks_per_tile, blocks_per_tile)
    q = ev_ref[here, 0].reshape(TILE, hd)
    g = ev_ref[here, 3].reshape(TILE, hd)
    start = pl.multiple_of(step * TILE, TILE)
    kw = k_all[pl.ds(start, span)]
    vw = v_all[pl.ds(start, span)]
    mk = mem_ref[:, 0].reshape(-1, hd)
    mv = mem_ref[:, 1].reshape(-1, hd)

    qpos = base + start + lax.broadcasted_iota(jnp.int32, (TILE, span), 0)
    kpos = base + start - WINDOW + lax.broadcasted_iota(jnp.int32, (TILE, span), 1)
    allowed = (
        (kpos <= qpos)
        & (qpos - kpos < WINDOW)
        & (kpos >= 0)
        & ((kpos < length) | (kpos == qpos))
    )
    per_source = mem_ref.shape[2]
    memory = mk.shape[0]
    which = lax.rem(lax.broadcasted_iota(jnp.int32, (1, memory), 1), per_source) // depth
    live = which < count

    sw = jnp.where(allowed, dot_nt(q, kw), NEG)
    sm = jnp.where(live, dot_nt(q, mk), NEG)
    top = jnp.maximum(
        jnp.max(sw, axis=1, keepdims=True), jnp.max(sm, axis=1, keepdims=True)
    )
    ew = jnp.exp2((sw - top) * slope)
    em = jnp.exp2((sm - top) * slope)
    dw = dot_nt(g, vw)
    dm = dot_nt(g, mv)
    total = jnp.sum(ew, axis=1, keepdims=True) + jnp.sum(em, axis=1, keepdims=True)
    inv = 1.0 / total
    delta = (
        jnp.sum(ew * dw, axis=1, keepdims=True) + jnp.sum(em * dm, axis=1, keepdims=True)
    ) * inv
    pw = ew * inv
    dsw = (pw * (dw - delta)).astype(jnp.bfloat16)
    dsm = (em * (dm - delta)).astype(jnp.bfloat16)
    gq = (dot_nn(dsw, kw) + dot_nn(dsm, mk) * inv) * scale
    gq_ref[pl.ds(step * blocks_per_tile, blocks_per_tile)] = gq.astype(gq_ref.dtype).reshape(
        blocks_per_tile, rows, hd
    )
    gk_ref[pl.ds(start, span)] += dot_tn(dsw, q) * scale
    gv_ref[pl.ds(start, span)] += dot_tn(pw.astype(jnp.bfloat16), g)
    if half == 0:
        stats_ref = refs[0]
        lane = lax.broadcasted_iota(jnp.int32, (TILE, hd), 1)
        both = jnp.where(lane == 0, top * slope + jnp.log2(total), delta)
        stats_ref[step] = both.T[:8]


def attend(scale, depth, half, seq_lengths, mem_counts, events, edge, memory):
    _, _, rows, hd = events.shape
    reach = WINDOW // rows
    keys = WINDOW + memory.shape[0] * memory.shape[2]
    whole = lambda shape: pl.BlockSpec(shape, lambda t: (0,) * len(shape))
    smem = pl.BlockSpec(memory_space=pltpu.SMEM)
    outs = [((reach, rows, hd), jnp.bfloat16)] + [((2 * WINDOW, hd), jnp.float32)] * 2
    if half == 0:
        outs.append(((WINDOW // TILE, 8, TILE), jnp.float32))
    return call(
        functools.partial(attend_body, scale, depth, half),
        grid=(WINDOW // TILE,),
        in_specs=[smem, smem, whole(events.shape), whole(edge.shape), whole(memory.shape)],
        out_specs=[whole(shape) for shape, _ in outs],
        out_shape=[jax.ShapeDtypeStruct(shape, dtype) for shape, dtype in outs],
        scratch_shapes=[pltpu.VMEM((2 * WINDOW, hd), jnp.bfloat16)] * 2,
        cost_estimate=pl.CostEstimate(
            flops=10 * WINDOW * keys * hd,
            bytes_accessed=4 * keys * hd,
            transcendentals=WINDOW * keys,
        ),
    )(seq_lengths, mem_counts, events, edge, memory)


def finish_body(scale, length_ref, ev_ref, edge_ref, stats_ref, *refs):
    (gq0, gk0, gv0, gq1, gk1, gv1), out_ref = refs[:-1], refs[-1]
    group, _, rows, hd = ev_ref.shape
    reach = WINDOW // rows
    early = group - reach
    number = lax.axis_index("seq") // H
    length = length_ref[lax.axis_index("dp")]
    follows = number + 1 < lax.axis_size("seq") // H
    base = number * (H * rows)
    slope = scale * LOG2E
    span = group * rows

    def put(where, part, value):
        out_ref[where, part] = value.astype(out_ref.dtype).reshape(reach, rows, hd)

    first, last = slice(0, early), slice(early, group)
    out_ref[first, 0] = gq0[...]
    out_ref[last, 0] = gq1[...]
    put(first, 1, gk0[WINDOW:] + gk1[:WINDOW])
    put(first, 2, gv0[WINDOW:] + gv1[:WINDOW])
    k = ev_ref[early:, 1].reshape(WINDOW, hd)
    v = ev_ref[early:, 2].reshape(WINDOW, hd)
    gk = jnp.zeros((WINDOW, hd), jnp.float32)
    gv = jnp.zeros((WINDOW, hd), jnp.float32)
    kpos = base + span - WINDOW + lax.broadcasted_iota(jnp.int32, (WINDOW, TILE), 0)
    for tile in range(WINDOW // TILE):
        blocks = slice(early + tile * TILE // rows, early + (tile + 1) * TILE // rows)
        q = edge_ref[blocks, 0].reshape(TILE, hd)
        g = edge_ref[blocks, 1].reshape(TILE, hd)
        qpos = base + span + tile * TILE + lax.broadcasted_iota(jnp.int32, (WINDOW, TILE), 1)
        allowed = (qpos - kpos < WINDOW) & (kpos < length) & follows
        s = jnp.where(allowed, dot_nt(k, q) * slope - stats_ref[tile, 0:1], NEG)
        p = jnp.exp2(s)
        d = dot_nt(v, g)
        ds = p * (d - stats_ref[tile, 1:2])
        gk += dot_nn(ds.astype(jnp.bfloat16), q)
        gv += dot_nn(p.astype(jnp.bfloat16), g)
    put(last, 1, gk1[WINDOW:] + gk * scale)
    put(last, 2, gv1[WINDOW:] + gv)


def finish(scale, seq_lengths, events, edge, stats, halves):
    group, _, rows, hd = events.shape
    vmem = pl.BlockSpec(memory_space=pltpu.VMEM)
    return call(
        functools.partial(finish_body, scale),
        in_specs=[pl.BlockSpec(memory_space=pltpu.SMEM)] + [vmem] * 9,
        out_specs=vmem,
        out_shape=jax.ShapeDtypeStruct((group, 3, rows, hd), jnp.bfloat16),
    )(seq_lengths, events, edge, stats, *halves)


def join_body(in_ref, *outs):
    hd = in_ref.shape[-1]
    for part, out_ref in enumerate(outs):
        for head in range(H):
            out_ref[0, :, head * hd : (head + 1) * hd] = in_ref[head, part]


def join_heads(pieces):
    heads, parts, rows, hd = pieces.shape
    vmem = pl.BlockSpec(memory_space=pltpu.VMEM)
    return call(
        join_body,
        in_specs=[vmem],
        out_specs=[vmem] * parts,
        out_shape=[jax.ShapeDtypeStruct((1, rows, heads * hd), pieces.dtype)] * parts,
    )(pieces)


def on_device(
    queries,
    keys,
    values,
    grad_out,
    mem_keys,
    mem_values,
    seq_lengths,
    mem_counts,
    block_lists,
    block_slots,
):
    rows, width = queries.shape[1:]
    scale = 1.0 / math.sqrt(width // H)
    reach = WINDOW // rows
    seq, users = lax.axis_size("seq"), lax.axis_size("dp")
    groups = [[first + i for i in range(H)] for first in range(0, seq, H)]
    swap = functools.partial(
        lax.all_to_all, axis_name="seq", split_axis=0, concat_axis=0, tiled=True
    )

    sent, edge = pack(
        users, block_slots, block_lists, queries, keys, values, grad_out, mem_keys, mem_values
    )
    got = []
    for step in range(1, users):
        pairs = [(i, (i + step) % users) for i in range(users)]
        got.append(lax.ppermute(sent[step - 1 : step], "dp", pairs))
    pairs = [(i, i - reach if i % H < reach else i + reach) for i in range(seq)]
    edge = lax.ppermute(edge, "seq", [(i, j) for i, j in pairs if 0 <= j < seq])

    events = split_heads(seq_lengths, queries, keys, values, grad_out)
    events = swap(events, axis_index_groups=groups)
    pieces = memory_pieces(block_slots, block_lists, mem_keys, mem_values, got, seq)
    memory = swap(pieces)
    edge = swap(split_edge(seq_lengths, edge, pieces), axis_index_groups=groups)

    depth = mem_keys.shape[1]
    part = functools.partial(attend, scale, depth)
    *first, stats = part(0, seq_lengths, mem_counts, events, edge, memory)
    stats = lax.ppermute(stats, "seq", [(i + H, i) for i in range(seq - H)])
    second = part(1, seq_lengths, mem_counts, events, edge, memory)
    out = finish(scale, seq_lengths, events, edge, stats, [*first, *second])
    return tuple(join_heads(swap(out, axis_index_groups=groups)))


def solution(mesh):
    spread = P("dp", "seq", None)
    return jax.shard_map(
        on_device,
        mesh=mesh,
        in_specs=(spread,) * 6 + (P(),) * 4,
        out_specs=(spread,) * 3,
        check_vma=False,
    )
```

time: 378 us -> 149 us (0.39)
  the two profiles are of different devices: /device:TPU:4 before, /device:TPU:0 now
where the time goes in v1:
time: 149 us
  blocking collectives  63.5 us (43%)
  Pallas kernels  56.3 us (38%)
  waiting for transfers between devices  16.6 us (11%)
  starting transfers between devices  10.3 us (7%)
    pallas_call x1, Pallas kernels, pack(): call(pack_body, limit=VMEM_WHOLE, in_specs=[smem] * 2 + [hbm] * 6, out_sp...  33.7 us
    all_to_all x1, blocking collectives, on_device(): memory = swap(pieces)  29.9 us
    all_to_all x1, blocking collectives, on_device(): events = swap(events, axis_index_groups=groups)  18.1 us
    all_to_all x1, blocking collectives, on_device(): return tuple(join_heads(swap(out, axis_index_groups=groups)))  15.5 us
    pallas_call x2, Pallas kernels, attend(): call(functools.partial(attend_body, scale, depth, half), grid=(WINDOW //...  11.8 us
    ppermute x1, waiting for transfers between devices, on_device(): got.append(lax.ppermute(sent[step - 1:step], 'dp', pairs))  10.6 us
    all_to_all x1, waiting for transfers between devices, on_device(): edge = swap(split_edge(seq_lengths, edge, pieces), axis_index_groups=groups)  6 us
    all_to_all x1, starting transfers between devices, on_device(): edge = swap(split_edge(seq_lengths, edge, pieces), axis_index_groups=groups)  4.41 us
  transfers between devices with their start and end apart: 4, of which 2 were waited for; matrix products, arithmetic and copies ran while one was open for 0% of the time, Pallas kernels for 8%

profile of v1, /device:TPU:0, one launch (start us, length us, event | category | flops | bytes accessed | tf_op | source)
XLA Modules:
  0.0 148.6 jit_solution(18253845278309926150)
XLA Ops:
  0.6 33.7 %shard_map.122 = (bf16[1,4,2,32,1024]{4,3,2,1,0:T(8,128)(2,1)}, bf16[2,128,1024]{2,1,0:T(8,128)(2,1)}) custom-call(s32[16]{0:T(128)} %slots_ref.3, s32[2,4]{1,0:T(2,128)} %lists_ref.3, bf16[1,128,1024]{2,1,0:T(8,128)(2,1)} %q_ref.1, bf16[1,128,1024]{2,1,0:T(8,128)(2,1)} %k_ref.1, bf16[1,128,1024]{2,1,0:T(8,128)(2,1)} %v_ref.1, bf16[1,128,1024]{2,1,0:T(8,128)(2,1)} %g_ref.1, ...), custom_call_target="tpu_custom_call" | custom-call | tf_op jit(solution)/shard_map/pallas_call | solution.py:82
  34.3 3.0 %collective-permute-start.1 = (bf16[1,4,2,32,1024]{4,3,2,1,0:T(8,128)(2,1)}, bf16[1,4,2,32,1024]{4,3,2,1,0:T(8,128)(2,1)}, u32[]{:S(2)}, u32[]{:S(2)}) collective-permute-start(bf16[1,4,2,32,1024]{4,3,2,1,0:T(8,128)(2,1)} %get-tuple-element.13), channel_id=1, source_target_pairs={{0,16},{16,0},{1,17},{17,1},{2,18},{18,2},{3,19},{19,3},{4,20},{20... | collective-permute-start | bytes 1572872 | tf_op jit(solution)/shard_map/ppermute | solution.py:426
  37.3 0.0 copy-start.2
  37.3 1.6 %collective-permute-start = (bf16[2,128,1024]{2,1,0:T(8,128)(2,1)}, bf16[2,128,1024]{2,1,0:T(8,128)(2,1)}, u32[]{:S(2)}, u32[]{:S(2)}) collective-permute-start(bf16[2,128,1024]{2,1,0:T(8,128)(2,1)} %get-tuple-element.12), channel_id=1, source_target_pairs={{4,8},{5,9},{6,10},{7,11},{8,4},{9,5},{10,6},{11,7},{20,24},{21,25... | collective-permute-start | bytes 1572872 | tf_op jit(solution)/shard_map/ppermute | solution.py:428
  38.9 10.6 %collective-permute-done.1.refs_0_ = bf16[1,4,2,32,1024]{4,3,2,1,0:T(8,128)(2,1)} collective-permute-done((bf16[1,4,2,32,1024]{4,3,2,1,0:T(8,128)(2,1)}, bf16[1,4,2,32,1024]{4,3,2,1,0:T(8,128)(2,1)}, u32[]{:S(2)}, u32[]{:S(2)}) %collective-permute-start.1) | collective-permute-done | bytes 524320 | tf_op jit(solution)/shard_map/ppermute | solution.py:426
  49.6 2.8 %shard_map.123._ = bf16[16,2,128,128]{3,2,1,0:T(8,128)(2,1)} custom-call(s32[16]{0:T(128)} %slots_ref.3, s32[2,4]{1,0:T(2,128)} %lists_ref.3, bf16[8,32,1024]{2,1,0:T(8,128)(2,1)} %mk_ref.3, bf16[8,32,1024]{2,1,0:T(8,128)(2,1)} %mv_ref.3, bf16[1,4,2,32,1024]{4,3,2,1,0:T(8,128)(2,1)} %collective-permute-done.1.refs_0_), custom_call_target="tpu_custom_call" | custom-call | tf_op jit(solution)/shard_map/pallas_call | solution.py:132
  52.4 0.0 collective-permute-done.in_ref
  52.4 0.0 copy-done.2
  52.4 0.0 copy-start
  52.4 1.2 copy-done
  53.7 1.9 %shard_map.124 = bf16[8,2,128,128]{3,2,1,0:T(8,128)(2,1)} custom-call(s32[2]{0:T(128)S(1)} %copy-done.2, bf16[2,128,1024]{2,1,0:T(8,128)(2,1)} %collective-permute-done.in_ref, bf16[16,2,128,128]{3,2,1,0:T(8,128)(2,1)S(1)} %copy-done), custom_call_target="tpu_custom_call" | custom-call | tf_op jit(solution)/shard_map/pallas_call | solution.py:201
  55.6 4.4 %all-to-all-start.1 = ((bf16[8,2,128,128]{3,2,1,0:T(8,128)(2,1)}), bf16[8,2,128,128]{3,2,1,0:T(8,128)(2,1)}, u32[]{:S(2)}, u32[]{:S(2)}) async-start(bf16[8,2,128,128]{3,2,1,0:T(8,128)(2,1)} %shard_map.124), calls=%async_computation.1 | async-start | bytes 1048576 | tf_op jit(solution)/shard_map/all_to_all | solution.py:434
  60.0 2.9 %shard_map.121 = bf16[8,4,128,128]{3,2,1,0:T(8,128)(2,1)} custom-call(s32[2]{0:T(128)} %length_ref.9, bf16[1,128,1024]{2,1,0:T(8,128)(2,1)} %q_ref.1, bf16[1,128,1024]{2,1,0:T(8,128)(2,1)} %k_ref.1, bf16[1,128,1024]{2,1,0:T(8,128)(2,1)} %v_ref.1, bf16[1,128,1024]{2,1,0:T(8,128)(2,1)} %g_ref.1), custom_call_target="tpu_custom_call" | custom-call | tf_op jit(solution)/shard_map/pallas_call | solution.py:169
  63.0 0.0 copy-start.1
  63.0 6.0 %all-to-all-done.1.edge_ref = bf16[8,2,128,128]{3,2,1,0:T(8,128)(2,1)} async-done(((bf16[8,2,128,128]{3,2,1,0:T(8,128)(2,1)}), bf16[8,2,128,128]{3,2,1,0:T(8,128)(2,1)}, u32[]{:S(2)}, u32[]{:S(2)}) %all-to-all-start.1) | async-done | bytes 524320 | tf_op jit(solution)/shard_map/all_to_all | solution.py:434
  69.0 18.1 %all_to_all.20.ev_ref = bf16[8,4,128,128]{3,2,1,0:T(8,128)(2,1)S(1)} all-to-all(bf16[8,4,128,128]{3,2,1,0:T(8,128)(2,1)} %shard_map.121), channel_id=1, replica_groups={{0,1,2,3,4,5,6,7},{8,9,10,11,12,13,14,15},{16,17,18,19,20,21,22,23},{24..., dimensions={0} | all-to-all | bytes 2097152 | tf_op jit(solution)/shard_map/all_to_all | solution.py:431
  87.0 0.0 copy-done.1
  87.0 0.0 copy-start.3
  87.0 0.0 copy-start.4
  87.0 29.9 %all_to_all.21.mem_ref = bf16[16,2,128,128]{3,2,1,0:T(8,128)(2,1)S(1)} all-to-all(bf16[16,2,128,128]{3,2,1,0:T(8,128)(2,1)S(1)} %copy-done.1), channel_id=1, replica_groups=mesh['dp'=2,'seq'=16] {'seq'}, dimensions={0} | all-to-all | bytes 2097152 | tf_op jit(solution)/shard_map/all_to_all | solution.py:433
  116.9 0.0 copy-done.3
  116.9 0.0 copy-done.4
  116.9 5.9 %shard_map.125 = (bf16[4,128,128]{2,1,0:T(8,128)(2,1)S(1)}, f32[1024,128]{1,0:T(8,128)S(1)}, f32[1024,128]{1,0:T(8,128)S(1)}, f32[2,8,256]{2,1,0:T(8,128)S(1)}) custom-call(s32[2]{0:T(128)S(1)} %copy-done.3, s32[2]{0:T(128)S(1)} %copy-done.4, bf16[8,4,128,128]{3,2,1,0:T(8,128)(2,1)S(1)} %all_to_all.20.ev_ref, ...), custom_call_target="tpu_custom_call" | custom-call | flops 1677721600 | bytes 1310720 | tf_op jit(solution)/shard_map/pallas_call | solution.py:314
  122.8 1.3 collective-permute-start.2
  124.1 5.9 %shard_map.126 = (bf16[4,128,128]{2,1,0:T(8,128)(2,1)S(1)}, f32[1024,128]{1,0:T(8,128)S(1)}, f32[1024,128]{1,0:T(8,128)S(1)}) custom-call(s32[2]{0:T(128)S(1)} %copy-done.3, s32[2]{0:T(128)S(1)} %copy-done.4, bf16[8,4,128,128]{3,2,1,0:T(8,128)(2,1)S(1)} %all_to_all.20.ev_ref, bf16[8,2,128,128]{3,2,1,0:T(8,128)(2,1)} %all-to-all-done.1.edge_ref, ...), custom_call_target="tpu_custom_call" | custom-call | flops 1677721600 | bytes 1310720 | tf_op jit(solution)/shard_map/pallas_call | solution.py:314
  130.1 0.0 collective-permute-done.2.stats_ref
  130.1 1.9 %shard_map.127 = bf16[8,3,128,128]{3,2,1,0:T(8,128)(2,1)S(1)} custom-call(s32[2]{0:T(128)S(1)} %copy-done.3, bf16[8,4,128,128]{3,2,1,0:T(8,128)(2,1)S(1)} %all_to_all.20.ev_ref, bf16[8,2,128,128]{3,2,1,0:T(8,128)(2,1)} %all-to-all-done.1.edge_ref, f32[2,8,256]{2,1,0:T(8,128)S(1)} %collective-permute-done.2.stats_ref, ...), custom_call_target="tpu_custom_call" | custom-call | tf_op jit(solution)/shard_map/pallas_call | solution.py:373
  132.1 15.5 %all_to_all.22.in_ref = bf16[8,3,128,128]{3,2,1,0:T(8,128)(2,1)S(1)} all-to-all(bf16[8,3,128,128]{3,2,1,0:T(8,128)(2,1)S(1)} %shard_map.127), channel_id=1, replica_groups={{0,1,2,3,4,5,6,7},{8,9,10,11,12,13,14,15},{16,17,18,19,20,21,22,23},{24..., dimensions={0} | all-to-all | bytes 1572864 | tf_op jit(solution)/shard_map/all_to_all | solution.py:442
  147.5 1.1 shard_map.128
Async XLA Ops:
  34.3 15.2 %collective-permute-start.1 = (bf16[1,4,2,32,1024]{4,3,2,1,0:T(8,128)(2,1)}, bf16[1,4,2,32,1024]{4,3,2,1,0:T(8,128)(2,1)}, u32[]{:S(2)}, u32[]{:S(2)}) collective-permute-start(bf16[1,4,2,32,1024]{4,3,2,1,0:T(8,128)(2,1)} %get-tuple-element.13), channel_id=1, source_target_pairs={{0,16},{16,0},{1,17},{17,1},{2,18},{18,2},{3,19},{19,3},{4,20},{20... | collective-permute-start | bytes 1572872 | tf_op jit(solution)/shard_map/ppermute | solution.py:426
  37.3 15.1 %copy-start.2 = (s32[2]{0:T(128)S(1)}, s32[2]{0:T(128)}, u32[]{:S(2)}) copy-start(s32[2]{0:T(128)} %length_ref.9) | copy-start | bytes 28
  37.3 15.1 %collective-permute-start = (bf16[2,128,1024]{2,1,0:T(8,128)(2,1)}, bf16[2,128,1024]{2,1,0:T(8,128)(2,1)}, u32[]{:S(2)}, u32[]{:S(2)}) collective-permute-start(bf16[2,128,1024]{2,1,0:T(8,128)(2,1)} %get-tuple-element.12), channel_id=1, source_target_pairs={{4,8},{5,9},{6,10},{7,11},{8,4},{9,5},{10,6},{11,7},{20,24},{21,25... | collective-permute-start | bytes 1572872 | tf_op jit(solution)/shard_map/ppermute | solution.py:428
  52.4 1.2 copy-start
  55.6 13.4 %all-to-all-start.1 = ((bf16[8,2,128,128]{3,2,1,0:T(8,128)(2,1)}), bf16[8,2,128,128]{3,2,1,0:T(8,128)(2,1)}, u32[]{:S(2)}, u32[]{:S(2)}) async-start(bf16[8,2,128,128]{3,2,1,0:T(8,128)(2,1)} %shard_map.124), calls=%async_computation.1 | async-start | bytes 1048576 | tf_op jit(solution)/shard_map/all_to_all | solution.py:434
  63.0 24.1 %copy-start.1 = (bf16[16,2,128,128]{3,2,1,0:T(8,128)(2,1)S(1)}, bf16[16,2,128,128]{3,2,1,0:T(8,128)(2,1)}, u32[]{:S(2)}) copy-start(bf16[16,2,128,128]{3,2,1,0:T(8,128)(2,1)} %shard_map.123._) | copy-start | bytes 3145732
  87.0 29.9 %copy-start.3 = (s32[2]{0:T(128)S(1)}, s32[2]{0:T(128)}, u32[]{:S(2)}) copy-start(s32[2]{0:T(128)} %length_ref.9) | copy-start | bytes 28
  87.0 29.9 %copy-start.4 = (s32[2]{0:T(128)S(1)}, s32[2]{0:T(128)}, u32[]{:S(2)}) copy-start(s32[2]{0:T(128)} %count_ref.3) | copy-start | bytes 28
  122.8 7.2 %collective-permute-start.2 = (f32[2,8,256]{2,1,0:T(8,128)S(1)}, f32[2,8,256]{2,1,0:T(8,128)S(1)}, u32[]{:S(2)}, u32[]{:S(2)}) collective-permute-start(f32[2,8,256]{2,1,0:T(8,128)S(1)} %get-tuple-element.14), channel_id=1, source_target_pairs={{8,0},{9,1},{10,2},{11,3},{12,4},{13,5},{14,6},{15,7},{24,16},{25,... | collective-permute-start | bytes 49160 | tf_op jit(solution)/shard_map/ppermute | solution.py:439
